TPU v7x, 128 devices: a whole 4x4x4 slice. The times are simulated.
128 devices in a mesh: rows: 128 (over y, x, z, core).
Axes of the slice: x: 4, y: 4, z: 4, core: 2. Of those that a mesh axis runs over, the one named last changes fastest.
Arguments:
- hologram: float32 [2, 65536, 1024], P(None, 'rows'), may hold values from -6 to 6
- phase: float32 [32768, 1024], P('rows'), may hold values from -3.140625 to 3.140625
- kept_blocks: int32 [512], replicated, may hold values from 0 to 1023, as said below
Outputs:
- propagated: float32 [2, 32768, 1024], P(None, 'rows')
Inputs may be any that keep to these rules, and one draw needn't show every extreme that they name: `kept_blocks`: distinct block indices; blocks 0 and 1023 are always kept.
All inputs are finite; a program needn't handle non-finite values.
Results may differ from a plain program's by a relative error of at most 0.00013.
Values sent between devices are 32-bit elements; how exact they have to be, the bound alone decides.
A program may use at most 64 MiB of HBM per device.

v0:
```python
import math

import jax
import jax.numpy as jnp
from jax import lax
from jax.sharding import PartitionSpec as P

BLK = 64


def partner_2(block, axis, stride):
    count = lax.axis_size(axis)
    route = []
    for low in range(count):
        high = low | 1 << stride
        if high != low and high < count:
            route += [(low, high), (high, low)]
    return lax.ppermute(block, axis, route)


def rotate_by(real_part, imag_part, angle_val):
    cosine = jnp.cos(angle_val)
    sine = jnp.sin(angle_val)
    return (real_part * cosine + imag_part * sine, imag_part * cosine - real_part * sine)


def reverse_bits(value, sections):
    result = jnp.zeros_like(value)
    for bit_pos in range(sections):
        result = result + value // 2**bit_pos % 2 * 2 ** (sections - 1 - bit_pos)
    return result


def local(hologram, phase, kept_blocks):
    axis_len = lax.axis_size("rows")
    position = lax.axis_index("rows")
    rows_dev = hologram.shape[1]
    length_all = rows_dev * axis_len
    sections = axis_len.bit_length() - 1
    two_pi = 2.0 * math.pi
    highest = lax.Precision.HIGHEST
    data = hologram
    for section in range(sections):
        bit_pos = sections - 1 - section
        half_span = 1 << bit_pos
        partner = partner_2(data, "rows", bit_pos)
        is_upper = position // half_span % 2
        offset = position % half_span
        angle_dev = two_pi * offset.astype(jnp.float32) / (2.0 * half_span)
        summed = data + partner
        difference = partner - data
        rot_re, rot_im = rotate_by(difference[0], difference[1], angle_dev)
        rotated = jnp.stack([rot_re, rot_im])
        data = jnp.where(is_upper == 1, rotated, summed)
    freq_low = reverse_bits(position, sections)
    local_rows = jnp.arange(rows_dev, dtype=jnp.int32)
    twiddle_angle = two_pi * (local_rows * freq_low % length_all).astype(jnp.float32) / length_all
    tw_re, tw_im = rotate_by(data[0], data[1], twiddle_angle[:, None])
    dft_angle = (
        two_pi
        * (local_rows[:, None] * local_rows[None, :] % rows_dev).astype(jnp.float32)
        / rows_dev
    )
    cos_local = jnp.cos(dft_angle)
    sin_local = jnp.sin(dft_angle)
    spec_re = jnp.dot(cos_local, tw_re, precision=highest) + jnp.dot(
        sin_local, tw_im, precision=highest
    )
    spec_im = jnp.dot(cos_local, tw_im, precision=highest) - jnp.dot(
        sin_local, tw_re, precision=highest
    )
    spectrum = jnp.stack([spec_re, spec_im])
    kept_all = kept_blocks.shape[0]
    kept_dev = kept_all // axis_len
    slots = max(1, BLK // axis_len)
    slot_ids = jnp.arange(slots, dtype=jnp.int32)
    first_off = (freq_low - kept_blocks * BLK) % axis_len
    within = first_off[:, None] + slot_ids[None, :] * axis_len
    usable = within < BLK
    freq_ids = kept_blocks[:, None] * BLK + within
    row_pick = jnp.where(usable, freq_ids // axis_len, 0).reshape(-1)
    send_rows = jnp.take(spectrum, row_pick, axis=1) * usable.reshape(1, -1, 1).astype(jnp.float32)
    received = lax.all_to_all(send_rows, "rows", split_axis=1, concat_axis=1, tiled=True)
    my_blocks = lax.dynamic_slice_in_dim(kept_blocks, position * kept_dev, kept_dev)
    block_off = jnp.arange(BLK, dtype=jnp.int32)
    out_freq = my_blocks[:, None] * BLK + block_off[None, :]
    residue = out_freq % axis_len
    source_dev = reverse_bits(residue, sections)
    block_pos = jnp.arange(kept_dev, dtype=jnp.int32)[:, None]
    recv_index = (
        source_dev * (kept_dev * slots) + block_pos * slots + block_off[None, :] // axis_len
    ).reshape(-1)
    chosen = jnp.take(received, recv_index, axis=1)
    scale_all = 1.0 / math.sqrt(length_all)
    cosine = jnp.cos(phase)
    sine = jnp.sin(phase)
    out_re = (chosen[0] * cosine - chosen[1] * sine) * scale_all
    out_im = (chosen[0] * sine + chosen[1] * cosine) * scale_all
    return jnp.stack([out_re, out_im])


def solution(mesh):
    in_specs = (P(None, "rows", None), P("rows", None), P())
    out_specs = P(None, "rows", None)
    return jax.shard_map(local, mesh=mesh, in_specs=in_specs, out_specs=out_specs, check_vma=False)
```

profile of v0, /device:TPU:1, one launch (start us, length us, event | category | flops | bytes accessed | tf_op | source)
XLA Modules:
  0.0 777.1 jit_solution(13018523773967102408)
XLA Ops:
  3.9 90.1 %collective-permute-done = f32[2,512,1024]{2,1,0:T(8,128)} collective-permute-done((f32[2,512,1024]{2,1,0:T(8,128)}, f32[2,512,1024]{2,1,0:T(8,128)}, u32[]{:S(2)}, u32[]{:S(2)}) %collective-permute-start) | collective-permute-done | bytes 4194336 | tf_op jit(solution)/shard_map/ppermute | solution.py:18
  94.1 4.4 sub.161
  100.7 5.7 maximum_select_fusion
  107.8 89.4 %collective-permute-done.1 = f32[2,512,1024]{2,1,0:T(8,128)} collective-permute-done((f32[2,512,1024]{2,1,0:T(8,128)}, f32[2,512,1024]{2,1,0:T(8,128)}, u32[]{:S(2)}, u32[]{:S(2)}) %collective-permute-start.1) | collective-permute-done | bytes 4194336 | tf_op jit(solution)/shard_map/ppermute | solution.py:18
  197.2 4.4 sub.163
  202.2 6.9 maximum_select_fusion.1
  212.0 88.5 %collective-permute-done.2 = f32[2,512,1024]{2,1,0:T(8,128)} collective-permute-done((f32[2,512,1024]{2,1,0:T(8,128)}, f32[2,512,1024]{2,1,0:T(8,128)}, u32[]{:S(2)}, u32[]{:S(2)}) %collective-permute-start.2) | collective-permute-done | bytes 4194336 | tf_op jit(solution)/shard_map/ppermute | solution.py:18
  300.6 4.4 sub.165
  305.6 6.9 maximum_select_fusion.2
  314.3 87.7 %collective-permute-done.3 = f32[2,512,1024]{2,1,0:T(8,128)} collective-permute-done((f32[2,512,1024]{2,1,0:T(8,128)}, f32[2,512,1024]{2,1,0:T(8,128)}, u32[]{:S(2)}, u32[]{:S(2)}) %collective-permute-start.3) | collective-permute-done | bytes 4194336 | tf_op jit(solution)/shard_map/ppermute | solution.py:18
  402.0 4.4 sub.167
  407.0 6.9 maximum_select_fusion.3
  417.6 86.7 %collective-permute-done.4 = f32[2,512,1024]{2,1,0:T(8,128)} collective-permute-done((f32[2,512,1024]{2,1,0:T(8,128)}, f32[2,512,1024]{2,1,0:T(8,128)}, u32[]{:S(2)}, u32[]{:S(2)}) %collective-permute-start.4) | collective-permute-done | bytes 4194336 | tf_op jit(solution)/shard_map/ppermute | solution.py:18
  504.3 4.4 sub.169
  509.3 6.9 maximum_select_fusion.4
  517.1 86.5 %collective-permute-done.5 = f32[2,512,1024]{2,1,0:T(8,128)} collective-permute-done((f32[2,512,1024]{2,1,0:T(8,128)}, f32[2,512,1024]{2,1,0:T(8,128)}, u32[]{:S(2)}, u32[]{:S(2)}) %collective-permute-start.5) | collective-permute-done | bytes 4194336 | tf_op jit(solution)/shard_map/ppermute | solution.py:18
  603.6 4.4 sub.171
  608.6 6.9 maximum_select_fusion.5
  615.6 6.0 collective-permute-start.6
  621.7 7.0 collective-permute-done.6
  633.6 5.0 maximum_select_fusion.6
  638.6 7.6 fusion.18
  646.2 7.8 %fusion.16 = f32[512,1024]{1,0:T(8,128)S(1)} fusion(f32[2,512,1024]{2,1,0:T(8,128)S(1)} %maximum_select_fusion.6, f32[512]{0:T(512)S(1)} %get-tuple-element.28, f32[512]{0:T(512)S(1)} %get-tuple-element.29), kind=kOutput, calls=%fused_computation.53 | convolution fusion | flops 3226468352 | bytes 6295552 | tf_op jit(solution)/shard_map/dot_general | solution.py:69
  654.0 8.0 %add_bitcast_fusion = f32[1,512,1024]{2,1,0:T(8,128)S(1)} fusion(f32[512,1024]{1,0:T(8,128)S(1)} %fusion.18, f32[2,512,1024]{2,1,0:T(8,128)S(1)} %maximum_select_fusion.6, f32[512]{0:T(512)S(1)} %get-tuple-element.28, f32[512]{0:T(512)S(1)} %get-tuple-element.29), kind=kOutput, calls=%fused_computation.16 | convolution fusion | flops 3226992640 | bytes 8392704 | tf_op jit(solution)/shard_map/dot_general | solution.py:66
  662.1 7.6 subtract_bitcast_fusion
  670.2 5.4 copy.4
  675.6 21.9 %gather_fusion = f32[512,2,1024]{2,1,0:T(2,128)} fusion(f32[2,512,1024]{2,0,1:T(2,128)} %copy.4, s32[1024]{0:T(1024)S(1)} %pad_clamp_fusion.1), kind=kCustom, calls=%fused_computation | custom fusion | bytes 8390656 | tf_op jit(solution)/shard_map/jit(_take)/gather | solution.py:82
  697.5 6.1 multiply_bitcast_fusion
  703.7 10.3 %all-to-all-start = ((f32[2,512,1024]{2,0,1:T(2,128)}), f32[2,512,1024]{2,0,1:T(2,128)}, u32[]{:S(2)}, u32[]{:S(2)}) async-start(f32[2,512,1024]{2,0,1:T(2,128)} %multiply_bitcast_fusion), calls=%async_computation | async-start | bytes 8388608 | tf_op jit(solution)/shard_map/all_to_all | solution.py:83
  714.8 4.4 fusion.85
  719.2 47.2 %all-to-all-done = f32[2,512,1024]{2,0,1:T(2,128)} async-done(((f32[2,512,1024]{2,0,1:T(2,128)}), f32[2,512,1024]{2,0,1:T(2,128)}, u32[]{:S(2)}, u32[]{:S(2)}) %all-to-all-start) | async-done | bytes 4194336 | tf_op jit(solution)/shard_map/all_to_all | solution.py:83
  766.5 5.0 gather_fusion.1
  (45 shorter events, 30.3 us)
Async XLA Ops:
  0.0 94.1 %collective-permute-start = (f32[2,512,1024]{2,1,0:T(8,128)}, f32[2,512,1024]{2,1,0:T(8,128)}, u32[]{:S(2)}, u32[]{:S(2)}) collective-permute-start(f32[2,512,1024]{2,1,0:T(8,128)} %param.3), channel_id=1, source_target_pairs={{0,64},{64,0},{1,65},{65,1},{2,66},{66,2},{3,67},{67,3},{4,68},{68... | collective-permute-start | bytes 12582920 | tf_op jit(solution)/shard_map/ppermute | solution.py:18
  98.5 2.2 copy-start
  106.3 90.9 %collective-permute-start.1 = (f32[2,512,1024]{2,1,0:T(8,128)}, f32[2,512,1024]{2,1,0:T(8,128)}, u32[]{:S(2)}, u32[]{:S(2)}) collective-permute-start(f32[2,512,1024]{2,1,0:T(8,128)} %maximum_select_fusion), channel_id=1, source_target_pairs={{0,32},{32,0},{1,33},{33,1},{2,34},{34,2},{3,35},{35,3},{4,36},{36... | collective-permute-start | bytes 12582920 | tf_op jit(solution)/shard_map/ppermute | solution.py:18
  209.1 91.4 %collective-permute-start.2 = (f32[2,512,1024]{2,1,0:T(8,128)}, f32[2,512,1024]{2,1,0:T(8,128)}, u32[]{:S(2)}, u32[]{:S(2)}) collective-permute-start(f32[2,512,1024]{2,1,0:T(8,128)} %maximum_select_fusion.1), channel_id=1, source_target_pairs={{0,16},{16,0},{1,17},{17,1},{2,18},{18,2},{3,19},{19,3},{4,20},{20... | collective-permute-start | bytes 12582920 | tf_op jit(solution)/shard_map/ppermute | solution.py:18
  312.5 89.5 %collective-permute-start.3 = (f32[2,512,1024]{2,1,0:T(8,128)}, f32[2,512,1024]{2,1,0:T(8,128)}, u32[]{:S(2)}, u32[]{:S(2)}) collective-permute-start(f32[2,512,1024]{2,1,0:T(8,128)} %maximum_select_fusion.2), channel_id=1, source_target_pairs={{0,8},{8,0},{1,9},{9,1},{2,10},{10,2},{3,11},{11,3},{4,12},{12,4},... | collective-permute-start | bytes 12582920 | tf_op jit(solution)/shard_map/ppermute | solution.py:18
  413.9 90.4 %collective-permute-start.4 = (f32[2,512,1024]{2,1,0:T(8,128)}, f32[2,512,1024]{2,1,0:T(8,128)}, u32[]{:S(2)}, u32[]{:S(2)}) collective-permute-start(f32[2,512,1024]{2,1,0:T(8,128)} %maximum_select_fusion.3), channel_id=1, source_target_pairs={{0,4},{4,0},{1,5},{5,1},{2,6},{6,2},{3,7},{7,3},{8,12},{12,8},{9,1... | collective-permute-start | bytes 12582920 | tf_op jit(solution)/shard_map/ppermute | solution.py:18
  516.2 87.4 %collective-permute-start.5 = (f32[2,512,1024]{2,1,0:T(8,128)}, f32[2,512,1024]{2,1,0:T(8,128)}, u32[]{:S(2)}, u32[]{:S(2)}) collective-permute-start(f32[2,512,1024]{2,1,0:T(8,128)} %maximum_select_fusion.4), channel_id=1, source_target_pairs={{0,2},{2,0},{1,3},{3,1},{4,6},{6,4},{5,7},{7,5},{8,10},{10,8},{9,1... | collective-permute-start | bytes 12582920 | tf_op jit(solution)/shard_map/ppermute | solution.py:18
  608.6 13.0 %copy-start.3 = (s32[512]{0:T(512)S(1)}, s32[512]{0:T(512)}, u32[]{:S(2)}) copy-start(s32[512]{0:T(512)} %param.5) | copy-start | bytes 6148
  615.6 13.2 %collective-permute-start.6 = (f32[2,512,1024]{2,1,0:T(8,128)}, f32[2,512,1024]{2,1,0:T(8,128)}, u32[]{:S(2)}, u32[]{:S(2)}) collective-permute-start(f32[2,512,1024]{2,1,0:T(8,128)} %maximum_select_fusion.5), channel_id=1, source_target_pairs={{0,1},{1,0},{2,3},{3,2},{4,5},{5,4},{6,7},{7,6},{8,9},{9,8},{10,11... | collective-permute-start | bytes 12582920 | tf_op jit(solution)/shard_map/ppermute | solution.py:18
  703.7 11.1 %copy-start.2 = (f32[256,1024]{1,0:T(8,128)S(1)}, f32[256,1024]{1,0:T(8,128)}, u32[]{:S(2)}) copy-start(f32[256,1024]{1,0:T(8,128)} %param.4) | copy-start | bytes 3145732
  703.7 62.8 %all-to-all-start = ((f32[2,512,1024]{2,0,1:T(2,128)}), f32[2,512,1024]{2,0,1:T(2,128)}, u32[]{:S(2)}, u32[]{:S(2)}) async-start(f32[2,512,1024]{2,0,1:T(2,128)} %multiply_bitcast_fusion), calls=%async_computation | async-start | bytes 8388608 | tf_op jit(solution)/shard_map/all_to_all | solution.py:83
  773.0 1.6 copy-start.1
where the time goes:
time: 785 us; the launch traced here: 777 us
  waiting for transfers between devices  583 us (74%)
  other arithmetic  90.8 us (12%)
  local copies, waits for them, and re-layouts  40.4 us (5%)
  matrix products  31.1 us (4%)
  starting transfers between devices  30 us (4%)
    ppermute x7, waiting for transfers between devices, partner_2(): return lax.ppermute(block, axis, route)  536 us
    all_to_all x1, waiting for transfers between devices, local(): lax.all_to_all(send_rows, 'rows', split_axis=1, concat_axis=1, tiled=True)  47.2 us
    select_n x7, other arithmetic, local(): data = jnp.where(is_upper == 1, rotated, summed)  45.3 us
    sub x7, other arithmetic, local(): difference = partner - data  30.8 us
    gather x1, local copies, waits for them, and re-layouts, local(): jnp.take(spectrum, row_pick, axis=1)  21.9 us
    ppermute x7, starting transfers between devices, partner_2(): return lax.ppermute(block, axis, route)  19.7 us
  transfers between devices with their start and end apart: 8, of which 8 were waited for; matrix products, arithmetic and copies ran while one was open for 1% of the time, Pallas kernels for 0%

commit v1 on v0

v1 whole, which is shorter than its diff:
```python
import jax
import jax.numpy as jnp
import numpy as np
from jax import lax
from jax.experimental import pallas as pl
from jax.experimental.pallas import tpu as pltpu
from jax.sharding import PartitionSpec as P

MESH = pl.DeviceIdType.MESH
DEVS = 128
ROWS = 512
COLS = 1024
HALVES = 2
CPC = 4
RAD = 256
SPEC = 512 * 8
STEP = 37


def tables():
    def split(a):
        a = a.astype(np.float32)
        hi = a.astype(jnp.bfloat16)
        lo = (a - hi.astype(np.float32)).astype(jnp.bfloat16)
        return hi, lo

    def real_form(angle):
        cos, sin = np.cos(angle), np.sin(angle)
        return np.block([[cos, sin], [-sin, cos]])

    k = np.arange(RAD)
    m = np.concatenate([2 * np.arange(DEVS), 2 * np.arange(DEVS) + 1])
    first = real_form(2 * np.pi * (np.outer(k, m) % RAD) / RAD)
    second = real_form(2 * np.pi * (np.outer(k, k) % RAD) / RAD)
    out = []
    for mat in (first, second):
        hi, lo = split(mat)
        out.append(np.concatenate([hi, hi, lo], axis=1))
    angle = 2 * np.pi * np.outer(k, k) / (RAD * RAD)
    twiddle = np.stack([np.cos(angle), np.sin(angle)]) / RAD
    return out[0], out[1], twiddle.astype(np.float32)


def peer_of(me, i):
    i = lax.rem(i * STEP, DEVS)
    core = lax.rem(me + i, 2)
    z = lax.rem(lax.div(me, 2) + lax.div(i, 2), 4)
    x = lax.rem(lax.div(me, 8) + lax.div(i, 8), 4)
    y = lax.rem(lax.div(me, 32) + lax.div(i, 32), 4)
    return ((y * 4 + x) * 4 + z) * 2 + core


def split3(a, axis):
    hi = a.astype(jnp.bfloat16)
    lo = (a - hi.astype(jnp.float32)).astype(jnp.bfloat16)
    return jnp.concatenate([hi, lo, hi], axis=axis)


def aligned(v, m):
    return pl.multiple_of(v, m)


def kernel(
    x_hbm, phase_hbm, g1_hbm, g2_hbm, tw_hbm, kept, out_hbm,
    x_v, s_in, r_in, spec, s_out, r_out, cos_v, sin_v, g1, g2, tw, out_v,
    x_sem, t_sem, o_sem, ss_in, rs_in, ss_out, rs_out,
):
    me = lax.axis_index("rows")
    barrier = pltpu.get_barrier_semaphore()

    def greet(i, c):
        pl.semaphore_signal(
            barrier, inc=1, device_id=(peer_of(me, i),), device_id_type=MESH
        )
        return c

    lax.fori_loop(1, DEVS, greet, 0)

    x_copies = [
        pltpu.make_async_copy(
            x_hbm.at[:, :, pl.ds(h * 512, 512)], x_v.at[h], x_sem.at[h]
        )
        for h in range(HALVES)
    ]
    for copy in x_copies:
        copy.start()
    table_copies = [
        pltpu.make_async_copy(src, dst, t_sem.at[n])
        for n, (src, dst) in enumerate(
            [(phase_hbm, cos_v), (g1_hbm, g1), (g2_hbm, g2), (tw_hbm, tw)]
        )
    ]
    for copy in table_copies:
        copy.start()

    def prepare(h):
        x_copies[h].wait()
        for ri in range(2):

            def one(c4, c):
                block = x_v[h, ri, :, pl.ds(aligned(c4 * 128, 128), 128)].T
                for rq in range(4):
                    s_in[h, pl.ds(rq * 8 + ri * 4 + c4, DEVS, stride=32), :] = block[
                        :, rq * 128 : (rq + 1) * 128
                    ]
                return c

            lax.fori_loop(0, CPC, one, 0)

    def send_in(h):
        def one(i, c):
            p = peer_of(me, i)
            pltpu.make_async_remote_copy(
                src_ref=s_in.at[h, pl.ds(aligned(p * 32, 32), 32)],
                dst_ref=r_in.at[h, pl.ds(aligned(me * 32, 32), 32)],
                send_sem=ss_in.at[h],
                recv_sem=rs_in.at[h],
                device_id=(p,),
                device_id_type=MESH,
            ).start()
            return c

        lax.fori_loop(1, DEVS, one, 0)
        own = pl.ds(aligned(me * 32, 32), 32)
        r_in[h, own, :] = s_in[h, own, :]

    def wait_bytes(ref, sem, h, rows):
        part = ref.at[h, pl.ds(0, rows)]
        pltpu.make_async_copy(part, part, sem.at[h]).wait()

    prepare(0)
    pl.semaphore_wait(barrier, DEVS - 1)
    send_in(0)
    prepare(1)
    send_in(1)

    table_copies[0].wait()

    def trig(i, c):
        rows = pl.ds(aligned(i * 8, 8), 8)
        angle = cos_v[rows, :]
        cos_v[rows, :] = jnp.cos(angle)
        sin_v[rows, :] = jnp.sin(angle)
        return c

    lax.fori_loop(0, 32, trig, 0)
    for copy in table_copies[1:]:
        copy.wait()

    flat = spec.reshape(2 * SPEC, 128)

    def transform(h):
        def one(c4, c):
            parts = []
            for ri in range(2):
                for rh in range(2):
                    parts.append(
                        jnp.concatenate(
                            [
                                r_in[
                                    h,
                                    pl.ds(
                                        (rh * 2 + rl) * 8 + ri * 4 + c4,
                                        DEVS,
                                        stride=32,
                                    ),
                                    :,
                                ]
                                for rl in range(2)
                            ],
                            axis=1,
                        )
                    )
            a = split3(jnp.concatenate(parts, axis=0), 0)
            y = jnp.dot(g1[...], a, preferred_element_type=jnp.float32)
            y_re, y_im = y[:RAD], y[RAD:]
            t_re, t_im = tw[0], tw[1]
            b = jnp.concatenate(
                [y_re * t_re + y_im * t_im, y_im * t_re - y_re * t_im], axis=1
            )
            z = lax.dot_general(
                g2[...],
                split3(b, 1),
                (((1,), (1,)), ((), ())),
                preferred_element_type=jnp.float32,
            )
            for ro in range(2):
                for kh in range(2):
                    tile = z[ro * RAD : (ro + 1) * RAD, kh * 128 : (kh + 1) * 128]
                    swapped = jnp.concatenate([tile[:, 64:], tile[:, :64]], axis=1)
                    row = kh * 8 + ro * 4 + c4
                    flat[pl.ds(row, RAD, stride=16), :] = tile
                    flat[pl.ds(SPEC + row, RAD, stride=16), :] = swapped
            return c

        lax.fori_loop(0, CPC, one, 0)

    low = lax.broadcasted_iota(jnp.int32, (8, 128), 1) < 64

    def gather(p):
        tiles = []
        for jp in range(2):
            halves = []
            for par in range(2):
                b = kept[p * 4 + jp * 2 + par]
                halves.append(spec[lax.div(b, 2) + lax.rem(b + par, 2) * 512])
            tiles.append(jnp.where(low, halves[0], halves[1]))
        return jnp.concatenate(tiles, axis=0)

    def send_out(h):
        def one(i, c):
            p = peer_of(me, i)
            mine = pl.ds(aligned(p * 16, 16), 16)
            s_out[h, mine, :] = gather(p)
            pltpu.make_async_remote_copy(
                src_ref=s_out.at[h, mine],
                dst_ref=r_out.at[h, pl.ds(aligned(me * 16, 16), 16)],
                send_sem=ss_out.at[h],
                recv_sem=rs_out.at[h],
                device_id=(p,),
                device_id_type=MESH,
            ).start()
            return c

        lax.fori_loop(1, DEVS, one, 0)
        r_out[h, pl.ds(aligned(me * 16, 16), 16), :] = gather(me)

    def finish(h):
        def one(c4, c):
            lanes = pl.ds(aligned((h * CPC + c4) * 128, 128), 128)
            for jp in range(2):
                rows = pl.ds(jp * 128, 128)
                re, im = [
                    r_out[h, pl.ds(jp * 8 + ri * 4 + c4, DEVS, stride=16), :].T
                    for ri in range(2)
                ]
                cos, sin = cos_v[rows, lanes], sin_v[rows, lanes]
                out_v[0, rows, lanes] = re * cos - im * sin
                out_v[1, rows, lanes] = re * sin + im * cos
            return c

        lax.fori_loop(0, CPC, one, 0)
        copy = pltpu.make_async_copy(
            out_v.at[:, :, pl.ds(h * 512, 512)],
            out_hbm.at[:, :, pl.ds(h * 512, 512)],
            o_sem.at[h],
        )
        copy.start()
        return copy

    for h in range(HALVES):
        wait_bytes(r_in, rs_in, h, (DEVS - 1) * 32)
        transform(h)
        send_out(h)
    out_copies = []
    for h in range(HALVES):
        wait_bytes(r_out, rs_out, h, (DEVS - 1) * 16)
        out_copies.append(finish(h))
    for h in range(HALVES):
        wait_bytes(s_in, ss_in, h, (DEVS - 1) * 32)
        wait_bytes(s_out, ss_out, h, (DEVS - 1) * 16)
        out_copies[h].wait()


def local(hologram, phase, kept_blocks):
    g1, g2, tw = tables()
    f32, bf16 = jnp.float32, jnp.bfloat16
    hbm = pl.BlockSpec(memory_space=pl.ANY)
    pair = pltpu.SemaphoreType.DMA((HALVES,))
    return pl.pallas_call(
        kernel,
        out_shape=jax.ShapeDtypeStruct((2, 256, COLS), f32),
        in_specs=[hbm] * 5 + [pl.BlockSpec(memory_space=pltpu.SMEM)],
        out_specs=hbm,
        scratch_shapes=[
            pltpu.VMEM((HALVES, 2, ROWS, COLS // HALVES), f32),
            pltpu.VMEM((HALVES, DEVS * 32, 128), f32),
            pltpu.VMEM((HALVES, DEVS * 32, 128), f32),
            pltpu.VMEM((2 * 512, 8, 128), f32),
            pltpu.VMEM((HALVES, DEVS * 16, 128), f32),
            pltpu.VMEM((HALVES, DEVS * 16, 128), f32),
            pltpu.VMEM((256, COLS), f32),
            pltpu.VMEM((256, COLS), f32),
            pltpu.VMEM(g1.shape, bf16),
            pltpu.VMEM(g2.shape, bf16),
            pltpu.VMEM(tw.shape, f32),
            pltpu.VMEM((2, 256, COLS), f32),
            pair,
            pltpu.SemaphoreType.DMA((4,)),
            pair, pair, pair, pair, pair,
        ],
        compiler_params=pltpu.CompilerParams(
            collective_id=0, has_side_effects=True, vmem_limit_bytes=48 << 20
        ),
    )(hologram, phase, jnp.asarray(g1), jnp.asarray(g2), jnp.asarray(tw), kept_blocks)


def solution(mesh):
    in_specs = (P(None, "rows", None), P("rows", None), P())
    out_specs = P(None, "rows", None)
    return jax.shard_map(local, mesh=mesh, in_specs=in_specs, out_specs=out_specs, check_vma=False)
```

time: 785 us -> 99.6 us (0.13)
  waiting for transfers between devices: 583 us -> 0 us
  other arithmetic: 90.8 us -> 0 us
  Pallas kernels: 0 us -> 90.4 us
  local copies, waits for them, and re-layouts: 40.4 us -> 8.92 us
  matrix products: 31.1 us -> 0 us
  starting transfers between devices: 30 us -> 0 us
    ppermute x7 -> x0, waiting for transfers between devices: 536 us -> none  [partner_2(): return lax.ppermute(block, axis, route)]
    pallas_call x0 -> x1, Pallas kernels: none -> 90.4 us  [local(): pl.pallas_call(kernel, out_shape=jax.ShapeDtypeStruct((2, 256, COLS), f32...]
    all_to_all x1 -> x0, waiting for transfers between devices: 47.2 us -> none  [local(): lax.all_to_all(send_rows, 'rows', split_axis=1, concat_axis=1, tiled=True)]
    select_n x10 -> x0, other arithmetic: 46.9 us -> none  [the longest x7 45.3 us: local(): data = jnp.where(is_upper == 1, rotated, summed)]
    dot_general x4 -> x0, matrix products: 31.1 us -> none  [the longest x1 8.05 us: local(): jnp.dot(cos_local, tw_re, precision=highest)]
    sub x7 -> x0, other arithmetic: 30.8 us -> none  [local(): difference = partner - data]
    gather x2 -> x0, local copies, waits for them, and re-layouts: 27 us -> none  [the longest x1 21.9 us: local(): jnp.take(spectrum, row_pick, axis=1)]
    ppermute x7 -> x0, starting transfers between devices: 19.7 us -> none  [partner_2(): return lax.ppermute(block, axis, route)]
  transfers between devices with their start and end apart: 8 -> 0, of which waited for: 8 -> 0; matrix products, arithmetic and copies ran while one was open for 1% -> 0% of each run, Pallas kernels for 0% -> 0%
where the time goes in v1:
time: 99.6 us; the launch traced here: 99.3 us
  Pallas kernels  90.4 us (91%)
  local copies, waits for them, and re-layouts  8.92 us (9%)
    pallas_call x1, Pallas kernels, local(): pl.pallas_call(kernel, out_shape=jax.ShapeDtypeStruct((2, 256, COLS), f32...  90.4 us
    unnamed x11, local copies, waits for them, and re-layouts  8.92 us

profile of v1, /device:TPU:1, one launch (start us, length us, event | category | flops | bytes accessed | tf_op | source)
XLA Modules:
  0.0 99.3 jit_solution(696571144455702559)
XLA Ops:
  0.0 0.0 copy-start
  0.0 1.4 %copy-done = bf16[512,1536]{1,0:T(8,128)(2,1)S(1)} copy-done((bf16[512,1536]{1,0:T(8,128)(2,1)S(1)}, bf16[512,1536]{1,0:T(8,128)(2,1)}, u32[]{:S(2)}) %copy-start) | copy-done | bytes 1572888
  1.4 0.0 copy-start.1
  1.4 1.4 %copy-done.1 = bf16[512,1536]{1,0:T(8,128)(2,1)S(1)} copy-done((bf16[512,1536]{1,0:T(8,128)(2,1)S(1)}, bf16[512,1536]{1,0:T(8,128)(2,1)}, u32[]{:S(2)}) %copy-start.1) | copy-done | bytes 1572888
  2.8 0.0 copy-start.2
  2.8 1.2 %copy-done.2 = f32[256,1024]{1,0:T(8,128)S(1)} copy-done((f32[256,1024]{1,0:T(8,128)S(1)}, f32[256,1024]{1,0:T(8,128)}, u32[]{:S(2)}) %copy-start.2) | copy-done | bytes 1048600
  4.0 0.0 copy-start.3
  4.0 1.0 %copy-done.3 = f32[2,256,256]{2,1,0:T(8,128)S(1)} copy-done((f32[2,256,256]{2,1,0:T(8,128)S(1)}, f32[2,256,256]{2,1,0:T(8,128)}, u32[]{:S(2)}) %copy-start.3) | copy-done | bytes 524312
  5.1 0.0 copy-start.4
  5.1 0.7 copy-done.4
  5.8 90.4 %shard_map.64 = f32[2,256,1024]{2,1,0:T(8,128)} custom-call(f32[2,512,1024]{2,1,0:T(8,128)} %x_hbm.1, f32[256,1024]{1,0:T(8,128)S(1)} %copy-done.2, bf16[512,1536]{1,0:T(8,128)(2,1)S(1)} %copy-done.1, bf16[512,1536]{1,0:T(8,128)(2,1)S(1)} %copy-done, f32[2,256,256]{2,1,0:T(8,128)S(1)} %copy-done.3, s32[512]{0:T(512)S(1)} %copy-done.4), custom_call_target="tpu_custom_call" | custom-call | tf_op jit(solution)/shard_map/pallas_call | solution.py:270
  96.2 3.2 %copy.8 = f32[2,256,1024]{2,1,0:T(8,128)} copy(f32[2,256,1024]{2,1,0:T(8,128)} %shard_map.64) | data formatting | bytes 4194304
Async XLA Ops:
  0.0 1.4 %copy-start = (bf16[512,1536]{1,0:T(8,128)(2,1)S(1)}, bf16[512,1536]{1,0:T(8,128)(2,1)}, u32[]{:S(2)}) copy-start(bf16[512,1536]{1,0:T(8,128)(2,1)} %constant.7.clone.g2_hbm) | copy-start | bytes 4718596
  1.4 1.4 %copy-start.1 = (bf16[512,1536]{1,0:T(8,128)(2,1)S(1)}, bf16[512,1536]{1,0:T(8,128)(2,1)}, u32[]{:S(2)}) copy-start(bf16[512,1536]{1,0:T(8,128)(2,1)} %constant.6.clone.g1_hbm) | copy-start | bytes 4718596
  2.8 1.2 %copy-start.2 = (f32[256,1024]{1,0:T(8,128)S(1)}, f32[256,1024]{1,0:T(8,128)}, u32[]{:S(2)}) copy-start(f32[256,1024]{1,0:T(8,128)} %phase_hbm.1) | copy-start | bytes 3145732
  4.0 1.0 %copy-start.3 = (f32[2,256,256]{2,1,0:T(8,128)S(1)}, f32[2,256,256]{2,1,0:T(8,128)}, u32[]{:S(2)}) copy-start(f32[2,256,256]{2,1,0:T(8,128)} %constant.8.clone.tw_hbm) | copy-start | bytes 1572868
  5.1 0.7 copy-start.4

commit v2 on v1

--- a/solution.py
+++ b/solution.py
@@ -41,13 +41,46 @@
     return out[0], out[1], twiddle.astype(np.float32)
 
 
+def shifted(me, dy, dx, dz, dc):
+    core = lax.rem(me + dc, 2)
+    z = lax.rem(lax.div(me, 2) + dz, 4)
+    x = lax.rem(lax.div(me, 8) + dx, 4)
+    y = lax.rem(lax.div(me, 32) + dy, 4)
+    return ((y * 4 + x) * 4 + z) * 2 + core
+
+
 def peer_of(me, i):
     i = lax.rem(i * STEP, DEVS)
-    core = lax.rem(me + i, 2)
-    z = lax.rem(lax.div(me, 2) + lax.div(i, 2), 4)
-    x = lax.rem(lax.div(me, 8) + lax.div(i, 8), 4)
-    y = lax.rem(lax.div(me, 32) + lax.div(i, 32), 4)
-    return ((y * 4 + x) * 4 + z) * 2 + core
+    return shifted(me, lax.div(i, 32), lax.div(i, 8), lax.div(i, 2), i)
+
+
+def turn(axis, u, v, w):
+    pick = lambda a, b, c: jnp.where(axis == 0, a, jnp.where(axis == 1, b, c))
+    return pick(u, w, v), pick(v, u, w), pick(w, v, u)
+
+
+def mate(me, i):
+    j = lax.div(i, 2)
+    far = 1 + lax.rem(lax.div(j, 3) + lax.rem(j, 3), 3)
+    far = jnp.where(i == 18, 0, far)
+    return shifted(me, *turn(lax.rem(j, 3), far, 0, 0), jnp.where(i == 18, 1, i))
+
+
+def corner(me, i):
+    j = lax.rem(i, 27)
+    k = lax.div(j, 3)
+    u = 1 + lax.rem(k, 3)
+    v = 1 + lax.rem(lax.div(k, 3) + k, 3)
+    return shifted(me, *turn(lax.rem(j, 3), u, v, 0), lax.div(i, 27))
+
+
+def opposite(me, i):
+    j = lax.rem(i, 27)
+    k = lax.div(j, 3)
+    u = lax.rem(j, 3)
+    v = lax.rem(u + k, 3)
+    w = lax.rem(u + 2 * k + lax.div(k, 3), 3)
+    return shifted(me, 1 + u, 1 + v, 1 + w, lax.div(i, 27))
 
 
 def split3(a, axis):
@@ -61,20 +94,21 @@
 
 
 def kernel(
-    x_hbm, phase_hbm, g1_hbm, g2_hbm, tw_hbm, kept, out_hbm,
-    x_v, s_in, r_in, spec, s_out, r_out, cos_v, sin_v, g1, g2, tw, out_v,
-    x_sem, t_sem, o_sem, ss_in, rs_in, ss_out, rs_out,
+    x_hbm, phase_hbm, g1_hbm, g2_hbm, tw_hbm, kept, out_v,
+    x_v, s_in, r_in, spec, s_out, r_out, cos_v, sin_v, g1, g2, tw,
+    x_sem, t_sem, round2, round3, ss_in, rs_in, ss_out, rs_out,
 ):
     me = lax.axis_index("rows")
     barrier = pltpu.get_barrier_semaphore()
 
+    def signal(sem, p):
+        pl.semaphore_signal(sem, inc=1, device_id=(p,), device_id_type=MESH)
+
     def greet(i, c):
-        pl.semaphore_signal(
-            barrier, inc=1, device_id=(peer_of(me, i),), device_id_type=MESH
-        )
+        signal(barrier, mate(me, i))
         return c
 
-    lax.fori_loop(1, DEVS, greet, 0)
+    lax.fori_loop(0, 19, greet, 0)
 
     x_copies = [
         pltpu.make_async_copy(
@@ -107,9 +141,9 @@
 
             lax.fori_loop(0, CPC, one, 0)
 
-    def send_in(h):
+    def send_in(h, group, count):
         def one(i, c):
-            p = peer_of(me, i)
+            p = group(me, i)
             pltpu.make_async_remote_copy(
                 src_ref=s_in.at[h, pl.ds(aligned(p * 32, 32), 32)],
                 dst_ref=r_in.at[h, pl.ds(aligned(me * 32, 32), 32)],
@@ -120,7 +154,9 @@
             ).start()
             return c
 
-        lax.fori_loop(1, DEVS, one, 0)
+        lax.fori_loop(0, count, one, 0)
+
+    def keep_own(h):
         own = pl.ds(aligned(me * 32, 32), 32)
         r_in[h, own, :] = s_in[h, own, :]
 
@@ -129,10 +165,23 @@
         pltpu.make_async_copy(part, part, sem.at[h]).wait()
 
     prepare(0)
-    pl.semaphore_wait(barrier, DEVS - 1)
-    send_in(0)
+    pl.semaphore_wait(barrier, 19)
+    for far in range(1, 4):
+        signal(round2, shifted(me, 0, far, 0, 0))
+        signal(round2, shifted(me, far, 0, 0, 0))
+    send_in(0, mate, 19)
+    pl.semaphore_wait(round2, 6)
+    for far in range(1, 4):
+        signal(round3, shifted(me, 0, far, 0, 0))
+    send_in(0, corner, 54)
     prepare(1)
-    send_in(1)
+    send_in(1, mate, 19)
+    pl.semaphore_wait(round3, 3)
+    send_in(0, opposite, 54)
+    send_in(1, corner, 54)
+    send_in(1, opposite, 54)
+    keep_own(0)
+    keep_own(1)
 
     table_copies[0].wait()
 
@@ -240,26 +289,17 @@
             return c
 
         lax.fori_loop(0, CPC, one, 0)
-        copy = pltpu.make_async_copy(
-            out_v.at[:, :, pl.ds(h * 512, 512)],
-            out_hbm.at[:, :, pl.ds(h * 512, 512)],
-            o_sem.at[h],
-        )
-        copy.start()
-        return copy
 
     for h in range(HALVES):
         wait_bytes(r_in, rs_in, h, (DEVS - 1) * 32)
         transform(h)
         send_out(h)
-    out_copies = []
     for h in range(HALVES):
         wait_bytes(r_out, rs_out, h, (DEVS - 1) * 16)
-        out_copies.append(finish(h))
+        finish(h)
     for h in range(HALVES):
         wait_bytes(s_in, ss_in, h, (DEVS - 1) * 32)
         wait_bytes(s_out, ss_out, h, (DEVS - 1) * 16)
-        out_copies[h].wait()
 
 
 def local(hologram, phase, kept_blocks):
@@ -269,9 +309,9 @@
     pair = pltpu.SemaphoreType.DMA((HALVES,))
     return pl.pallas_call(
         kernel,
-        out_shape=jax.ShapeDtypeStruct((2, 256, COLS), f32),
+        out_shape=pltpu.VMEM((2, 256, COLS), f32),
         in_specs=[hbm] * 5 + [pl.BlockSpec(memory_space=pltpu.SMEM)],
-        out_specs=hbm,
+        out_specs=pl.BlockSpec(memory_space=pltpu.VMEM),
         scratch_shapes=[
             pltpu.VMEM((HALVES, 2, ROWS, COLS // HALVES), f32),
             pltpu.VMEM((HALVES, DEVS * 32, 128), f32),
@@ -284,13 +324,14 @@
             pltpu.VMEM(g1.shape, bf16),
             pltpu.VMEM(g2.shape, bf16),
             pltpu.VMEM(tw.shape, f32),
-            pltpu.VMEM((2, 256, COLS), f32),
             pair,
             pltpu.SemaphoreType.DMA((4,)),
-            pair, pair, pair, pair, pair,
+            pltpu.SemaphoreType.REGULAR,
+            pltpu.SemaphoreType.REGULAR,
+            pair, pair, pair, pair,
         ],
         compiler_params=pltpu.CompilerParams(
-            collective_id=0, has_side_effects=True, vmem_limit_bytes=48 << 20
+            collective_id=0, has_side_effects=True, vmem_limit_bytes=61 << 20
         ),
     )(hologram, phase, jnp.asarray(g1), jnp.asarray(g2), jnp.asarray(tw), kept_blocks)
 

time: 99.6 us -> 87.5 us (0.88)
  local copies, waits for them, and re-layouts: 8.92 us -> 1.32 us
  Pallas kernels: 90.4 us -> 86 us
    unnamed x11 -> x1, local copies, waits for them, and re-layouts: 8.92 us -> 1.32 us
    pallas_call x1, Pallas kernels: 90.4 us -> 86 us  [local(): pl.pallas_call(kernel, out_shape=pltpu.VMEM((2, 256, COLS), f32), in_spec...]
where the time goes in v2:
time: 87.5 us; the launch traced here: 87.3 us
  Pallas kernels  86 us (98%)
  local copies, waits for them, and re-layouts  1.32 us (2%)
    pallas_call x1, Pallas kernels, local(): pl.pallas_call(kernel, out_shape=pltpu.VMEM((2, 256, COLS), f32), in_spec...  86 us

profile of v2, /device:TPU:1, one launch (start us, length us, event | category | flops | bytes accessed | tf_op | source)
XLA Modules:
  0.0 87.3 jit_solution(8140674879676938699)
XLA Ops:
  0.0 86.0 %shard_map.64 = f32[2,256,1024]{2,1,0:T(8,128)S(1)} custom-call(f32[2,512,1024]{2,1,0:T(8,128)} %x_hbm.1, f32[256,1024]{1,0:T(8,128)} %phase_hbm.1, bf16[512,1536]{1,0:T(8,128)(2,1)} %constant.6.clone.g1_hbm, bf16[512,1536]{1,0:T(8,128)(2,1)} %constant.7.clone.g2_hbm, f32[2,256,256]{2,1,0:T(8,128)} %constant.8.clone.tw_hbm, s32[512]{0:T(512)} %kept.1), custom_call_target="tpu_custom_call" | custom-call | tf_op jit(solution)/shard_map/pallas_call | solution.py:310
  86.0 1.3 %copy.8 = f32[2,256,1024]{2,1,0:T(8,128)} copy(f32[2,256,1024]{2,1,0:T(8,128)S(1)} %shard_map.64) | data formatting | bytes 4194304

commit v3 on v2

--- a/solution.py
+++ b/solution.py
@@ -14,7 +14,6 @@
 CPC = 4
 RAD = 256
 SPEC = 512 * 8
-STEP = 37
 
 
 def tables():
@@ -41,46 +40,28 @@
     return out[0], out[1], twiddle.astype(np.float32)
 
 
-def shifted(me, dy, dx, dz, dc):
-    core = lax.rem(me + dc, 2)
-    z = lax.rem(lax.div(me, 2) + dz, 4)
-    x = lax.rem(lax.div(me, 8) + dx, 4)
-    y = lax.rem(lax.div(me, 32) + dy, 4)
-    return ((y * 4 + x) * 4 + z) * 2 + core
-
-
-def peer_of(me, i):
-    i = lax.rem(i * STEP, DEVS)
-    return shifted(me, lax.div(i, 32), lax.div(i, 8), lax.div(i, 2), i)
-
-
-def turn(axis, u, v, w):
-    pick = lambda a, b, c: jnp.where(axis == 0, a, jnp.where(axis == 1, b, c))
-    return pick(u, w, v), pick(v, u, w), pick(w, v, u)
-
-
-def mate(me, i):
-    j = lax.div(i, 2)
-    far = 1 + lax.rem(lax.div(j, 3) + lax.rem(j, 3), 3)
-    far = jnp.where(i == 18, 0, far)
-    return shifted(me, *turn(lax.rem(j, 3), far, 0, 0), jnp.where(i == 18, 1, i))
-
-
-def corner(me, i):
-    j = lax.rem(i, 27)
-    k = lax.div(j, 3)
-    u = 1 + lax.rem(k, 3)
-    v = 1 + lax.rem(lax.div(k, 3) + k, 3)
-    return shifted(me, *turn(lax.rem(j, 3), u, v, 0), lax.div(i, 27))
-
-
-def opposite(me, i):
-    j = lax.rem(i, 27)
-    k = lax.div(j, 3)
-    u = lax.rem(j, 3)
-    v = lax.rem(u + k, 3)
-    w = lax.rem(u + 2 * k + lax.div(k, 3), 3)
-    return shifted(me, 1 + u, 1 + v, 1 + w, lax.div(i, 27))
+def shifts():
+    near = [(0, 0, 0, 1)]
+    near += [
+        tuple(far if a == axis else 0 for a in range(3)) + (core,)
+        for far in (1, 3, 2)
+        for axis in range(3)
+        for core in range(2)
+    ]
+    corner, opposite = [], []
+    for core in range(2):
+        for k in range(9):
+            u, v = 1 + k % 3, 1 + (k // 3 + k) % 3
+            corner += [(u, v, 0, core), (0, u, v, core), (v, 0, u, core)]
+        for j in range(27):
+            k, u = divmod(j, 3)
+            v, w = (u + k) % 3, (u + 2 * k + k // 3) % 3
+            opposite.append((1 + u, 1 + v, 1 + w, core))
+    return near + corner + opposite
+
+
+SHIFTS = shifts()
+MATES, CORNERS = 19, 54
 
 
 def split3(a, axis):
@@ -95,7 +76,7 @@
 
 def kernel(
     x_hbm, phase_hbm, g1_hbm, g2_hbm, tw_hbm, kept, out_v,
-    x_v, s_in, r_in, spec, s_out, r_out, cos_v, sin_v, g1, g2, tw,
+    peer, x_v, s_in, r_in, spec, s_out, r_out, cos_v, sin_v, g1, g2, tw,
     x_sem, t_sem, round2, round3, ss_in, rs_in, ss_out, rs_out,
 ):
     me = lax.axis_index("rows")
@@ -104,11 +85,18 @@
     def signal(sem, p):
         pl.semaphore_signal(sem, inc=1, device_id=(p,), device_id_type=MESH)
 
-    def greet(i, c):
-        signal(barrier, mate(me, i))
-        return c
-
-    lax.fori_loop(0, 19, greet, 0)
+    place = [lax.rem(lax.div(me, w), n) for w, n in ((32, 4), (8, 4), (2, 4), (1, 2))]
+    moved = [
+        [lax.rem(v + d, n) * w for d in range(n)]
+        for v, (w, n) in zip(place, ((32, 4), (8, 4), (2, 4), (1, 2)))
+    ]
+
+    def at(shift):
+        y, x, z, core = [moved[axis][d] for axis, d in enumerate(shift)]
+        return y + x + z + core
+
+    for shift in SHIFTS[:MATES]:
+        signal(barrier, at(shift))
 
     x_copies = [
         pltpu.make_async_copy(
@@ -141,9 +129,9 @@
 
             lax.fori_loop(0, CPC, one, 0)
 
-    def send_in(h, group, count):
+    def send_in(h, first, last):
         def one(i, c):
-            p = group(me, i)
+            p = peer[i]
             pltpu.make_async_remote_copy(
                 src_ref=s_in.at[h, pl.ds(aligned(p * 32, 32), 32)],
                 dst_ref=r_in.at[h, pl.ds(aligned(me * 32, 32), 32)],
@@ -154,7 +142,7 @@
             ).start()
             return c
 
-        lax.fori_loop(0, count, one, 0)
+        lax.fori_loop(first, last, one, 0)
 
     def keep_own(h):
         own = pl.ds(aligned(me * 32, 32), 32)
@@ -164,22 +152,25 @@
         part = ref.at[h, pl.ds(0, rows)]
         pltpu.make_async_copy(part, part, sem.at[h]).wait()
 
+    for i, shift in enumerate(SHIFTS):
+        peer[i] = at(shift)
     prepare(0)
-    pl.semaphore_wait(barrier, 19)
+    edge = MATES + CORNERS
+    pl.semaphore_wait(barrier, MATES)
     for far in range(1, 4):
-        signal(round2, shifted(me, 0, far, 0, 0))
-        signal(round2, shifted(me, far, 0, 0, 0))
-    send_in(0, mate, 19)
+        signal(round2, at((0, far, 0, 0)))
+        signal(round2, at((far, 0, 0, 0)))
+    send_in(0, 0, MATES)
+    prepare(1)
     pl.semaphore_wait(round2, 6)
     for far in range(1, 4):
-        signal(round3, shifted(me, 0, far, 0, 0))
-    send_in(0, corner, 54)
-    prepare(1)
-    send_in(1, mate, 19)
+        signal(round3, at((0, far, 0, 0)))
+    send_in(0, MATES, edge)
+    send_in(1, 0, MATES)
     pl.semaphore_wait(round3, 3)
-    send_in(0, opposite, 54)
-    send_in(1, corner, 54)
-    send_in(1, opposite, 54)
+    send_in(0, edge, DEVS - 1)
+    send_in(1, MATES, edge)
+    send_in(1, edge, DEVS - 1)
     keep_own(0)
     keep_own(1)
 
@@ -242,7 +233,7 @@
                     flat[pl.ds(SPEC + row, RAD, stride=16), :] = swapped
             return c
 
-        lax.fori_loop(0, CPC, one, 0)
+        lax.fori_loop(0, CPC, one, 0, unroll=4)
 
     low = lax.broadcasted_iota(jnp.int32, (8, 128), 1) < 64
 
@@ -258,7 +249,7 @@
 
     def send_out(h):
         def one(i, c):
-            p = peer_of(me, i)
+            p = peer[DEVS - 1 - i]
             mine = pl.ds(aligned(p * 16, 16), 16)
             s_out[h, mine, :] = gather(p)
             pltpu.make_async_remote_copy(
@@ -271,7 +262,7 @@
             ).start()
             return c
 
-        lax.fori_loop(1, DEVS, one, 0)
+        lax.fori_loop(1, DEVS, one, 0, unroll=4)
         r_out[h, pl.ds(aligned(me * 16, 16), 16), :] = gather(me)
 
     def finish(h):
@@ -288,7 +279,7 @@
                 out_v[1, rows, lanes] = re * sin + im * cos
             return c
 
-        lax.fori_loop(0, CPC, one, 0)
+        lax.fori_loop(0, CPC, one, 0, unroll=4)
 
     for h in range(HALVES):
         wait_bytes(r_in, rs_in, h, (DEVS - 1) * 32)
@@ -313,6 +304,7 @@
         in_specs=[hbm] * 5 + [pl.BlockSpec(memory_space=pltpu.SMEM)],
         out_specs=pl.BlockSpec(memory_space=pltpu.VMEM),
         scratch_shapes=[
+            pltpu.SMEM((DEVS,), jnp.int32),
             pltpu.VMEM((HALVES, 2, ROWS, COLS // HALVES), f32),
             pltpu.VMEM((HALVES, DEVS * 32, 128), f32),
             pltpu.VMEM((HALVES, DEVS * 32, 128), f32),

time: 87.5 us -> 85.3 us (0.975)
  Pallas kernels: 86 us -> 83.9 us
    pallas_call x1, Pallas kernels: 86 us -> 83.9 us  [local(): pl.pallas_call(kernel, out_shape=pltpu.VMEM((2, 256, COLS), f32), in_spec...]
where the time goes in v3:
time: 85.3 us; the launch traced here: 85.2 us
  Pallas kernels  83.9 us (98%)
  local copies, waits for them, and re-layouts  1.32 us (2%)
    pallas_call x1, Pallas kernels, local(): pl.pallas_call(kernel, out_shape=pltpu.VMEM((2, 256, COLS), f32), in_spec...  83.9 us

profile of v3, /device:TPU:1, one launch (start us, length us, event | category | flops | bytes accessed | tf_op | source)
XLA Modules:
  0.0 85.2 jit_solution(9251137663955365601)
XLA Ops:
  0.0 83.9 %shard_map.64 = f32[2,256,1024]{2,1,0:T(8,128)S(1)} custom-call(f32[2,512,1024]{2,1,0:T(8,128)} %x_hbm.1, f32[256,1024]{1,0:T(8,128)} %phase_hbm.1, bf16[512,1536]{1,0:T(8,128)(2,1)} %constant.6.clone.g1_hbm, bf16[512,1536]{1,0:T(8,128)(2,1)} %constant.7.clone.g2_hbm, f32[2,256,256]{2,1,0:T(8,128)} %constant.8.clone.tw_hbm, s32[512]{0:T(512)} %kept.1), custom_call_target="tpu_custom_call" | custom-call | tf_op jit(solution)/shard_map/pallas_call | solution.py:301
  83.9 1.3 %copy.8 = f32[2,256,1024]{2,1,0:T(8,128)} copy(f32[2,256,1024]{2,1,0:T(8,128)S(1)} %shard_map.64) | data formatting | bytes 4194304

commit v4 on v3

--- a/solution.py
+++ b/solution.py
@@ -169,8 +169,8 @@
     send_in(1, 0, MATES)
     pl.semaphore_wait(round3, 3)
     send_in(0, edge, DEVS - 1)
+    send_in(1, edge, DEVS - 1)
     send_in(1, MATES, edge)
-    send_in(1, edge, DEVS - 1)
     keep_own(0)
     keep_own(1)
 

time: 85.3 us -> 84.9 us (level)
  no operation moved by 1% of the time
where the time goes in v4:
time: 84.9 us; the launch traced here: 84.8 us
  Pallas kernels  83.4 us (98%)
  local copies, waits for them, and re-layouts  1.32 us (2%)
    pallas_call x1, Pallas kernels, local(): pl.pallas_call(kernel, out_shape=pltpu.VMEM((2, 256, COLS), f32), in_spec...  83.4 us

profile of v4, /device:TPU:1, one launch (start us, length us, event | category | flops | bytes accessed | tf_op | source)
XLA Modules:
  0.0 84.8 jit_solution(11903435423241668321)
XLA Ops:
  0.0 83.4 %shard_map.64 = f32[2,256,1024]{2,1,0:T(8,128)S(1)} custom-call(f32[2,512,1024]{2,1,0:T(8,128)} %x_hbm.1, f32[256,1024]{1,0:T(8,128)} %phase_hbm.1, bf16[512,1536]{1,0:T(8,128)(2,1)} %constant.6.clone.g1_hbm, bf16[512,1536]{1,0:T(8,128)(2,1)} %constant.7.clone.g2_hbm, f32[2,256,256]{2,1,0:T(8,128)} %constant.8.clone.tw_hbm, s32[512]{0:T(512)} %kept.1), custom_call_target="tpu_custom_call" | custom-call | tf_op jit(solution)/shard_map/pallas_call | solution.py:301
  83.4 1.3 %copy.8 = f32[2,256,1024]{2,1,0:T(8,128)} copy(f32[2,256,1024]{2,1,0:T(8,128)S(1)} %shard_map.64) | data formatting | bytes 4194304

commit v5 on v4

--- a/solution.py
+++ b/solution.py
@@ -154,18 +154,18 @@
 
     for i, shift in enumerate(SHIFTS):
         peer[i] = at(shift)
-    prepare(0)
     edge = MATES + CORNERS
     pl.semaphore_wait(barrier, MATES)
     for far in range(1, 4):
         signal(round2, at((0, far, 0, 0)))
         signal(round2, at((far, 0, 0, 0)))
+    prepare(0)
     send_in(0, 0, MATES)
-    prepare(1)
     pl.semaphore_wait(round2, 6)
     for far in range(1, 4):
         signal(round3, at((0, far, 0, 0)))
     send_in(0, MATES, edge)
+    prepare(1)
     send_in(1, 0, MATES)
     pl.semaphore_wait(round3, 3)
     send_in(0, edge, DEVS - 1)
@@ -249,7 +249,7 @@
 
     def send_out(h):
         def one(i, c):
-            p = peer[DEVS - 1 - i]
+            p = peer[lax.rem(edge + i - 1, DEVS - 1)]
             mine = pl.ds(aligned(p * 16, 16), 16)
             s_out[h, mine, :] = gather(p)
             pltpu.make_async_remote_copy(

time: 84.9 us -> 83.7 us (0.986)
  Pallas kernels: 83.4 us -> 82.2 us
    pallas_call x1, Pallas kernels: 83.4 us -> 82.2 us  [local(): pl.pallas_call(kernel, out_shape=pltpu.VMEM((2, 256, COLS), f32), in_spec...]
where the time goes in v5:
time: 83.7 us; the launch traced here: 83.5 us
  Pallas kernels  82.2 us (98%)
  local copies, waits for them, and re-layouts  1.32 us (2%)
    pallas_call x1, Pallas kernels, local(): pl.pallas_call(kernel, out_shape=pltpu.VMEM((2, 256, COLS), f32), in_spec...  82.2 us

profile of v5, /device:TPU:1, one launch (start us, length us, event | category | flops | bytes accessed | tf_op | source)
XLA Modules:
  0.0 83.5 jit_solution(12542827305900331535)
XLA Ops:
  0.0 82.2 %shard_map.64 = f32[2,256,1024]{2,1,0:T(8,128)S(1)} custom-call(f32[2,512,1024]{2,1,0:T(8,128)} %x_hbm.1, f32[256,1024]{1,0:T(8,128)} %phase_hbm.1, bf16[512,1536]{1,0:T(8,128)(2,1)} %constant.6.clone.g1_hbm, bf16[512,1536]{1,0:T(8,128)(2,1)} %constant.7.clone.g2_hbm, f32[2,256,256]{2,1,0:T(8,128)} %constant.8.clone.tw_hbm, s32[512]{0:T(512)} %kept.1), custom_call_target="tpu_custom_call" | custom-call | tf_op jit(solution)/shard_map/pallas_call | solution.py:301
  82.2 1.3 %copy.8 = f32[2,256,1024]{2,1,0:T(8,128)} copy(f32[2,256,1024]{2,1,0:T(8,128)S(1)} %shard_map.64) | data formatting | bytes 4194304

commit v6 on v5

--- a/solution.py
+++ b/solution.py
@@ -99,12 +99,15 @@
         signal(barrier, at(shift))
 
     x_copies = [
-        pltpu.make_async_copy(
-            x_hbm.at[:, :, pl.ds(h * 512, 512)], x_v.at[h], x_sem.at[h]
-        )
+        [
+            pltpu.make_async_copy(
+                x_hbm.at[ri, :, pl.ds(h * 512, 512)], x_v.at[h, ri], x_sem.at[h, ri]
+            )
+            for ri in range(2)
+        ]
         for h in range(HALVES)
     ]
-    for copy in x_copies:
+    for copy in x_copies[0] + x_copies[1]:
         copy.start()
     table_copies = [
         pltpu.make_async_copy(src, dst, t_sem.at[n])
@@ -116,8 +119,8 @@
         copy.start()
 
     def prepare(h):
-        x_copies[h].wait()
         for ri in range(2):
+            x_copies[h][ri].wait()
 
             def one(c4, c):
                 block = x_v[h, ri, :, pl.ds(aligned(c4 * 128, 128), 128)].T
@@ -127,7 +130,7 @@
                     ]
                 return c
 
-            lax.fori_loop(0, CPC, one, 0)
+            lax.fori_loop(0, CPC, one, 0, unroll=2)
 
     def send_in(h, first, last):
         def one(i, c):
@@ -316,7 +319,7 @@
             pltpu.VMEM(g1.shape, bf16),
             pltpu.VMEM(g2.shape, bf16),
             pltpu.VMEM(tw.shape, f32),
-            pair,
+            pltpu.SemaphoreType.DMA((HALVES, 2)),
             pltpu.SemaphoreType.DMA((4,)),
             pltpu.SemaphoreType.REGULAR,
             pltpu.SemaphoreType.REGULAR,

time: 83.7 us -> 83.6 us (level)
  no operation moved by 1% of the time
where the time goes in v6:
time: 83.6 us; the launch traced here: 83.5 us
  Pallas kernels  82.2 us (98%)
  local copies, waits for them, and re-layouts  1.32 us (2%)
    pallas_call x1, Pallas kernels, local(): pl.pallas_call(kernel, out_shape=pltpu.VMEM((2, 256, COLS), f32), in_spec...  82.2 us

profile of v6, /device:TPU:1, one launch (start us, length us, event | category | flops | bytes accessed | tf_op | source)
XLA Modules:
  0.0 83.5 jit_solution(17166414369741802129)
XLA Ops:
  0.0 82.2 %shard_map.64 = f32[2,256,1024]{2,1,0:T(8,128)S(1)} custom-call(f32[2,512,1024]{2,1,0:T(8,128)} %x_hbm.1, f32[256,1024]{1,0:T(8,128)} %phase_hbm.1, bf16[512,1536]{1,0:T(8,128)(2,1)} %constant.6.clone.g1_hbm, bf16[512,1536]{1,0:T(8,128)(2,1)} %constant.7.clone.g2_hbm, f32[2,256,256]{2,1,0:T(8,128)} %constant.8.clone.tw_hbm, s32[512]{0:T(512)} %kept.1), custom_call_target="tpu_custom_call" | custom-call | tf_op jit(solution)/shard_map/pallas_call | solution.py:304
  82.2 1.3 %copy.8 = f32[2,256,1024]{2,1,0:T(8,128)} copy(f32[2,256,1024]{2,1,0:T(8,128)S(1)} %shard_map.64) | data formatting | bytes 4194304
